TPU v7x, 32 devices: a whole 2x2x4 slice. The times are simulated.
32 devices in a mesh: row: 4 (over y, core), col: 8 (over z, x).
Axes of the slice: x: 2, y: 2, z: 4, core: 2. Of those that a mesh axis runs over, the one named last changes fastest.
Arguments:
- fronts: bfloat16 [8, 1024, 1024], P('col', 'row')
- pivots: int32 [8], replicated, may hold values from 1 to 3, as said below
- targets: int32 [8, 4], replicated, may hold values from 0 to 7, as said below
- ancestor: bfloat16 [2, 1024, 2048], P(None, 'row', 'col'), may hold values from -1.5 to 1.5
Outputs:
- factor: float32 [8, 1024, 768], P('col', 'row')
- assembled: float32 [2, 1024, 2048], P(None, 'row', 'col')
Inputs may be any that keep to these rules, and one draw needn't show every extreme that they name: `pivots`: every sibling eliminates at least one pivot block column; counts of 1 and of 3 both occur. targets[s, j] is j or j + 4; both ends of the range occur.
All inputs are finite; a program needn't handle non-finite values.
Results may differ from a plain program's by a relative error of at most 0.0011.
Values may be sent and summed in bfloat16 or wider, within the bound.
A program may use at most 128 MiB of HBM per device.

v0:
```python
import jax
import jax.numpy as jnp
from jax import lax
from jax.sharding import PartitionSpec as P

STEPS = 3


def broadcast(shard, axis, root):
    mine = lax.axis_index(axis) == root
    return lax.psum(jnp.where(mine, shard, jnp.zeros_like(shard)), axis)


def contract(left_rows, right_rows):
    return lax.dot_general(
        left_rows, right_rows, (((1,), (1,)), ((), ())), preferred_element_type=jnp.float32
    )


def shards(fronts, pivots, targets, ancestor):
    row_index = lax.axis_index("row")
    col_index = lax.axis_index("col")
    col_count = lax.axis_size("col")
    block_size = fronts.shape[1]
    width = fronts.shape[2]
    block_count = width // block_size
    sibling_ids = jnp.arange(pivots.shape[0], dtype=jnp.int32)
    pivot_count = jnp.sum(jnp.where(sibling_ids == col_index, pivots, 0))
    working = fronts[0].astype(jnp.float32)
    factor_blocks = []
    for section in range(STEPS):
        lower_edge = section * block_size
        upper_edge = lower_edge + block_size
        column_block = working[:, lower_edge:upper_edge]
        diagonal = broadcast(column_block, "row", section)
        lower_block = jnp.linalg.cholesky(diagonal)
        solved = jax.scipy.linalg.solve_triangular(lower_block, column_block.T, lower=True).T
        is_active = section < pivot_count
        own_block = jnp.where(
            row_index > section, solved, jnp.where(row_index == section, lower_block, 0.0)
        )
        factor_blocks.append(jnp.where(is_active, own_block, 0.0))
        outgoing = jnp.where(is_active & (row_index > section), solved, 0.0).astype(jnp.bfloat16)

        def panel_product(piece_rows, first_row, outgoing=outgoing):
            return contract(outgoing, piece_rows)

        working = working - panel_product(
            lax.all_gather(outgoing, "row", axis=0, tiled=True), jnp.int32(0)
        )
    factor = jnp.concatenate(factor_blocks, axis=1)[None]
    row_blocks = working.reshape(block_size, block_count, block_size)
    my_targets = jnp.sum(jnp.where(sibling_ids[:, None] == col_index, targets, 0), axis=0)
    dest_ids = jnp.arange(col_count, dtype=jnp.int32)
    source_ids = dest_ids % block_count
    owned_target = jnp.concatenate([my_targets, my_targets])
    keep = (owned_target == dest_ids) & (source_ids >= pivot_count) & (row_index >= pivot_count)
    outgoing_blocks = jnp.where(
        keep[None, :, None], jnp.concatenate([row_blocks, row_blocks], axis=1), 0.0
    )
    received = lax.all_to_all(outgoing_blocks, "col", split_axis=1, concat_axis=1, tiled=True)
    block_ids = jnp.arange(block_count, dtype=jnp.int32)
    row_targets = jnp.sum(jnp.where(block_ids[None, :] == row_index, targets, 0), axis=1)
    halves = row_targets // block_count
    selector = (halves[None, :] == jnp.arange(2, dtype=jnp.int32)[:, None]).astype(jnp.float32)
    summed = jnp.einsum("hc,tcb->htb", selector, received, precision=lax.Precision.HIGHEST)
    assembled = ancestor.astype(jnp.float32) + summed
    return (factor, assembled)


def solution(mesh):
    in_specs = (P("col", "row", None), P(), P(), P(None, "row", "col"))
    out_specs = (P("col", "row", None), P(None, "row", "col"))
    return jax.shard_map(shards, mesh=mesh, in_specs=in_specs, out_specs=out_specs, check_vma=False)
```

profile of v0, /device:TPU:15, one launch (start us, length us, event | category | flops | bytes accessed | tf_op | source)
XLA Modules:
  0.0 398.0 jit_solution(15360962862731837609)
XLA Ops:
  10.7 31.6 %all-reduce.5.cloned.1.call-done = f32[256,256]{0,1:T(8,128)} async-done(((f32[256,256]{0,1:T(8,128)}), f32[256,256]{0,1:T(8,128)}) %all-reduce.5.cloned.1.call-update) | async-done | bytes 262160 | tf_op jit(solution)/shard_map/psum | solution.py:11
  44.4 11.7 %cholesky.172 = f32[128,128]{1,0:T(8,128)S(1)} custom-call(f32[128,128]{1,0:T(8,128)S(1)} %cholesky.270), custom_call_target="Cholesky" | custom-call | tf_op jit(solution)/shard_map/jit(cholesky)/cholesky | solution.py:36
  56.2 9.8 %custom-call.15 = f32[1,128,128]{1,2,0:T(8,128)S(1)} custom-call(f32[1,128,128]{2,1,0:T(8,128)S(1)} %get-tuple-element.98), custom_call_target="InvertDiagBlocksLowerTriangular" | custom-call | tf_op jit(solution)/shard_map/jit(cholesky)/cholesky | solution.py:36
  66.6 11.7 %cholesky.189 = f32[128,128]{1,0:T(8,128)S(1)} custom-call(f32[128,128]{1,0:T(8,128)S(1)} %convolution_subtract_fusion.8), custom_call_target="Cholesky" | custom-call | tf_op jit(solution)/shard_map/jit(cholesky)/cholesky | solution.py:36
  80.7 4.6 %while.6 = (s32[]{:T(128)}, f32[256,256]{0,1:T(8,128)S(1)}, s32[2,2]{1,0:T(2,128)S(1)}, f32[2,128,128]{2,1,0:T(8,128)S(1)}, s32[]{:T(128)}) while((s32[]{:T(128)}, f32[256,256]{0,1:T(8,128)S(1)}, s32[2,2]{1,0:T(2,128)S(1)}, f32[2,128,128]{2,1,0:T(8,128)S(1)}, s32[]{:T(128)}) %tuple.73), condition=%wide.while_cond, body=%wide.while_body.sunk | while | flops 2 | bytes 393329 | solution.py:37
  85.3 19.7 %custom-call.16 = f32[2,128,128]{1,2,0:T(8,128)S(1)} custom-call(f32[2,128,128]{2,1,0:T(8,128)S(1)} %get-tuple-element.24), custom_call_target="InvertDiagBlocksLowerTriangular" | custom-call | tf_op jit(solution)/shard_map/jit(_solve_triangular)/triangular_solve | solution.py:37
  106.0 8.5 %all_gather.9 = bf16[1024,256]{0,1:T(8,128)(2,1)S(1)} all-gather(bf16[256,256]{0,1:T(8,128)(2,1)S(1)} %select_convert_fusion.2), channel_id=1, replica_groups=mesh['row'=4,'col'=8] {'row'}, dimensions={0}, use_global_device_ids=true | all-gather | bytes 655360 | tf_op jit(solution)/shard_map/all_gather | solution.py:49
  116.3 30.1 %all-reduce.7.cloned.1.call-done = f32[256,256]{0,1:T(8,128)} async-done(((f32[256,256]{0,1:T(8,128)}), f32[256,256]{0,1:T(8,128)}) %all-reduce.7.cloned.1.call-update) | async-done | bytes 262160 | tf_op jit(solution)/shard_map/psum | solution.py:11
  148.5 11.7 %cholesky.206 = f32[128,128]{1,0:T(8,128)S(1)} custom-call(f32[128,128]{1,0:T(8,128)S(1)} %cholesky.273), custom_call_target="Cholesky" | custom-call | tf_op jit(solution)/shard_map/jit(cholesky)/cholesky | solution.py:36
  160.3 9.8 %custom-call.17 = f32[1,128,128]{1,2,0:T(8,128)S(1)} custom-call(f32[1,128,128]{2,1,0:T(8,128)S(1)} %get-tuple-element.96), custom_call_target="InvertDiagBlocksLowerTriangular" | custom-call | tf_op jit(solution)/shard_map/jit(cholesky)/cholesky | solution.py:36
  170.7 11.7 %cholesky.223 = f32[128,128]{1,0:T(8,128)S(1)} custom-call(f32[128,128]{1,0:T(8,128)S(1)} %convolution_subtract_fusion.7), custom_call_target="Cholesky" | custom-call | tf_op jit(solution)/shard_map/jit(cholesky)/cholesky | solution.py:36
  185.4 14.5 %while.7 = (s32[]{:T(128)}, f32[256,256]{0,1:T(8,128)S(1)}, s32[2,2]{1,0:T(2,128)S(1)}, f32[2,128,128]{2,1,0:T(8,128)S(1)}, s32[]{:T(128)}) while((s32[]{:T(128)}, f32[256,256]{0,1:T(8,128)S(1)}, s32[2,2]{1,0:T(2,128)S(1)}, f32[2,128,128]{2,1,0:T(8,128)S(1)}, s32[]{:T(128)}) %tuple.88), condition=%wide.while_cond.clone, body=%wide.while_body.clone.sunk | while | flops 2 | bytes 393329 | solution.py:37
  199.9 19.7 %custom-call.18 = f32[2,128,128]{1,2,0:T(8,128)S(1)} custom-call(f32[2,128,128]{2,1,0:T(8,128)S(1)} %get-tuple-element.25), custom_call_target="InvertDiagBlocksLowerTriangular" | custom-call | tf_op jit(solution)/shard_map/jit(_solve_triangular)/triangular_solve | solution.py:37
  220.6 8.6 %all_gather.10 = bf16[1024,256]{0,1:T(8,128)(2,1)S(1)} all-gather(bf16[256,256]{0,1:T(8,128)(2,1)S(1)} %select_convert_fusion.1), channel_id=1, replica_groups=mesh['row'=4,'col'=8] {'row'}, dimensions={0}, use_global_device_ids=true | all-gather | bytes 655360 | tf_op jit(solution)/shard_map/all_gather | solution.py:49
  232.4 28.7 %all-reduce.9.cloned.1.call-done = f32[256,256]{0,1:T(8,128)} async-done(((f32[256,256]{0,1:T(8,128)}), f32[256,256]{0,1:T(8,128)}) %all-reduce.9.cloned.1.call-update) | async-done | bytes 262160 | tf_op jit(solution)/shard_map/psum | solution.py:11
  263.2 11.7 %cholesky.240 = f32[128,128]{1,0:T(8,128)S(1)} custom-call(f32[128,128]{1,0:T(8,128)S(1)} %cholesky.276), custom_call_target="Cholesky" | custom-call | tf_op jit(solution)/shard_map/jit(cholesky)/cholesky | solution.py:36
  275.0 9.8 %custom-call.19 = f32[1,128,128]{1,2,0:T(8,128)S(1)} custom-call(f32[1,128,128]{2,1,0:T(8,128)S(1)} %get-tuple-element.94), custom_call_target="InvertDiagBlocksLowerTriangular" | custom-call | tf_op jit(solution)/shard_map/jit(cholesky)/cholesky | solution.py:36
  285.5 11.7 %cholesky.257 = f32[128,128]{1,0:T(8,128)S(1)} custom-call(f32[128,128]{1,0:T(8,128)S(1)} %convolution_subtract_fusion.6), custom_call_target="Cholesky" | custom-call | tf_op jit(solution)/shard_map/jit(cholesky)/cholesky | solution.py:36
  300.1 4.6 %while.8 = (s32[]{:T(128)}, f32[256,256]{0,1:T(8,128)S(1)}, s32[2,2]{1,0:T(2,128)S(1)}, f32[2,128,128]{2,1,0:T(8,128)S(1)}, s32[]{:T(128)}) while((s32[]{:T(128)}, f32[256,256]{0,1:T(8,128)S(1)}, s32[2,2]{1,0:T(2,128)S(1)}, f32[2,128,128]{2,1,0:T(8,128)S(1)}, s32[]{:T(128)}) %tuple.89), condition=%wide.while_cond.clone.1, body=%wide.while_body.clone.1.sunk | while | flops 2 | bytes 393329 | solution.py:37
  304.6 19.7 %custom-call.20 = f32[2,128,128]{1,2,0:T(8,128)S(1)} custom-call(f32[2,128,128]{2,1,0:T(8,128)S(1)} %get-tuple-element.26), custom_call_target="InvertDiagBlocksLowerTriangular" | custom-call | tf_op jit(solution)/shard_map/jit(_solve_triangular)/triangular_solve | solution.py:37
  325.9 8.5 %all_gather.11 = bf16[1024,256]{0,1:T(8,128)(2,1)S(1)} all-gather(bf16[256,256]{0,1:T(8,128)(2,1)S(1)} %select_convert_fusion), channel_id=1, replica_groups=mesh['row'=4,'col'=8] {'row'}, dimensions={0}, use_global_device_ids=true | all-gather | bytes 655360 | tf_op jit(solution)/shard_map/all_gather | solution.py:49
  336.7 5.6 %all-to-all-start = ((f32[256,8,256]{2,0,1:T(8,128)}), f32[256,8,256]{2,0,1:T(8,128)S(1)}, u32[]{:S(2)}, u32[]{:S(2)}) async-start(f32[256,8,256]{2,0,1:T(8,128)} %maximum_select_fusion), calls=%async_computation | async-start | bytes 4194304 | tf_op jit(solution)/shard_map/all_to_all | solution.py:61
  344.6 43.4 %all-to-all-done = f32[256,8,256]{2,0,1:T(8,128)S(1)} async-done(((f32[256,8,256]{2,0,1:T(8,128)}), f32[256,8,256]{2,0,1:T(8,128)S(1)}, u32[]{:S(2)}, u32[]{:S(2)}) %all-to-all-start) | async-done | bytes 2097184 | tf_op jit(solution)/shard_map/all_to_all | solution.py:61
  388.0 2.4 fusion.2
  (128 shorter events, 40.0 us)
Async XLA Ops:
  7.2 2.2 copy-start.5
  7.2 35.1 %all-reduce.5.cloned.1.call-start = ((), (), s32[]{:S(2)}) async-start(), calls=%async_computation.1 | async-start | bytes 524288 | tf_op jit(solution)/shard_map/psum | solution.py:11
  9.3 137.1 %all-reduce.7.cloned.1.call-start = ((), (), s32[]{:S(2)}) async-start(), calls=%async_computation.2 | async-start | bytes 524288 | tf_op jit(solution)/shard_map/psum | solution.py:11
  115.6 145.5 %all-reduce.9.cloned.1.call-start = ((), (), s32[]{:S(2)}) async-start(), calls=%async_computation.3 | async-start | bytes 524288 | tf_op jit(solution)/shard_map/psum | solution.py:11
  220.5 9.8 %copy-start = (f32[128,256]{1,0:T(8,128)}, f32[128,256]{1,0:T(8,128)S(1)}, u32[]{:S(2)}) copy-start(f32[128,256]{1,0:T(8,128)S(1)} %fusion.23) | copy-start | bytes 393220
  220.5 9.7 %copy-start.4 = (s32[8,4]{0,1:T(4,128)S(1)}, s32[8,4]{0,1:T(4,128)}, u32[]{:S(2)}) copy-start(s32[8,4]{0,1:T(4,128)} %param.9) | copy-start | bytes 388
  325.3 0.7 copy-start.2
  336.7 5.7 %copy-start.1 = (f32[128,256]{1,0:T(8,128)S(1)}, f32[128,256]{1,0:T(8,128)}, u32[]{:S(2)}) copy-start(f32[128,256]{1,0:T(8,128)} %copy-done) | copy-start | bytes 393220
  336.7 51.3 %all-to-all-start = ((f32[256,8,256]{2,0,1:T(8,128)}), f32[256,8,256]{2,0,1:T(8,128)S(1)}, u32[]{:S(2)}, u32[]{:S(2)}) async-start(f32[256,8,256]{2,0,1:T(8,128)} %maximum_select_fusion), calls=%async_computation | async-start | bytes 4194304 | tf_op jit(solution)/shard_map/all_to_all | solution.py:61
  343.4 44.6 %copy-start.3 = (bf16[2,256,256]{2,1,0:T(8,128)(2,1)S(1)}, bf16[2,256,256]{2,1,0:T(8,128)(2,1)}, u32[]{:S(2)}) copy-start(bf16[2,256,256]{2,1,0:T(8,128)(2,1)} %param.10) | copy-start | bytes 786436
Sparse Core Ops, SparseCore 0:
  10.9 31.3 all-reduce.4
  115.7 30.6 all-reduce.6
  230.4 30.6 all-reduce.8
where the time goes:
time: 406 us; the launch traced here: 398 us
  other arithmetic  172 us (42%)
  waiting for transfers between devices  134 us (33%)
  blocking collectives  25.6 us (6%)
  between operations  21.2 us (5%)
  local copies, waits for them, and re-layouts  21 us (5%)
  loops' own time  10.9 us (3%)
  matrix products  7.87 us (2%)
  starting transfers between devices  5.73 us (1%)
    another operation x20, other arithmetic, shards(): lower_block = jnp.linalg.cholesky(diagonal)  103 us
    psum x3, waiting for transfers between devices, broadcast(): return lax.psum(jnp.where(mine, shard, jnp.zeros_like(shard)), axis)  90.3 us
    another operation x7, other arithmetic, shards(): jax.scipy.linalg.solve_triangular(lower_block, column_block.T, lower=True)  59.1 us
    all_to_all x1, waiting for transfers between devices, shards(): lax.all_to_all(outgoing_blocks, 'col', split_axis=1, concat_axis=1, tiled...  43.4 us
    all_gather x3, blocking collectives, shards(): lax.all_gather(outgoing, 'row', axis=0, tiled=True)  25.6 us
    another operation x34, local copies, waits for them, and re-layouts, shards(): jax.scipy.linalg.solve_triangular(lower_block, column_block.T, lower=True)  12.9 us
    another operation x3, loops' own time, shards(): jax.scipy.linalg.solve_triangular(lower_block, column_block.T, lower=True)  10.9 us
  transfers between devices with their start and end apart: 4, of which 4 were waited for; matrix products, arithmetic and copies ran while one was open for 1% of the time, Pallas kernels for 0%

commit v1 on v0

v1 whole, which is shorter than its diff:
```python
import functools

import jax
import jax.numpy as jnp
from jax import lax
from jax.experimental import pallas as pl
from jax.experimental.pallas import tpu as pltpu
from jax.sharding import PartitionSpec as P

STEPS = 3
BASE = 128
GROUP = 8
F32 = jnp.float32
BF16 = jnp.bfloat16


def split(x):
    high = x.astype(BF16)
    return high, (x - high.astype(F32)).astype(BF16)


def dot3(a, b, dims):
    a_high, a_low = split(a)
    b_high, b_low = split(b)

    def one(x, y):
        return lax.dot_general(x, y, (dims, ((), ())), preferred_element_type=F32)

    return one(a_high, b_high) + (one(a_high, b_low) + one(a_low, b_high))


def splat(x, i, j):
    return jnp.broadcast_to(x[i : i + 1, j : j + 1], (GROUP, BASE))


def row_of(x, i):
    return jnp.broadcast_to(x[i : i + 1, :], (GROUP, BASE))


def column_of(x, j):
    return jnp.broadcast_to(x[:, j : j + 1], (GROUP, BASE))


def factor_base(matrix):
    count = BASE // GROUP
    sub = lax.broadcasted_iota(jnp.int32, (GROUP, BASE), 0)
    lane = lax.broadcasted_iota(jnp.int32, (GROUP, BASE), 1)
    left = [matrix[m * GROUP : (m + 1) * GROUP, :] for m in range(count)]
    right = [(lane == sub + m * GROUP).astype(F32) for m in range(count)]
    upper, inverse = [], []
    for g in range(count):
        first = g * GROUP
        s = {
            (i, j): splat(left[g], i, first + j)
            for i in range(GROUP)
            for j in range(i, GROUP)
        }
        rows = [row_of(left[g], i) for i in range(GROUP)]
        extra = [row_of(right[g], i) for i in range(GROUP)]
        scale, u = [], {}
        for i in range(GROUP):
            r = lax.rsqrt(s[i, i])
            scale.append(r)
            for j in range(i + 1, GROUP):
                u[i, j] = s[i, j] * r
            rows[i] = rows[i] * r
            extra[i] = extra[i] * r
            for j in range(i + 1, GROUP):
                for k in range(j, GROUP):
                    s[j, k] = s[j, k] - u[i, j] * u[i, k]
                rows[j] = rows[j] - u[i, j] * rows[i]
                extra[j] = extra[j] - u[i, j] * extra[i]
        top, bottom = rows[0], extra[0]
        for i in range(1, GROUP):
            top = jnp.where(sub == i, rows[i], top)
            bottom = jnp.where(sub == i, extra[i], bottom)
        upper.append(jnp.where(lane >= sub + first, top, 0.0))
        inverse.append(bottom)
        if g + 1 == count:
            break
        m = g + 1
        left_sum, right_sum = left[m], right[m]
        columns = [column_of(left[m], first + i) for i in range(GROUP)]
        for i in range(GROUP):
            columns[i] = columns[i] * scale[i]
            for j in range(i + 1, GROUP):
                columns[j] = columns[j] - u[i, j] * columns[i]
            left_sum = left_sum - columns[i] * rows[i]
            right_sum = right_sum - columns[i] * extra[i]
        left[m], right[m] = left_sum, right_sum
        if g + 2 == count:
            continue
        back, back_extra = [None] * GROUP, [None] * GROUP
        for i in reversed(range(GROUP)):
            a, b = rows[i], extra[i]
            for k in range(i + 1, GROUP):
                a = a - u[i, k] * back[k]
                b = b - u[i, k] * back_extra[k]
            back[i], back_extra[i] = a * scale[i], b * scale[i]
        for m in range(g + 2, count):
            left_sum, right_sum = left[m], right[m]
            for i in range(GROUP):
                column = column_of(left[m], first + i)
                left_sum = left_sum - column * back[i]
                right_sum = right_sum - column * back_extra[i]
            left[m], right[m] = left_sum, right_sum
    return jnp.concatenate(upper, axis=0), jnp.concatenate(inverse, axis=0)


def front_kernel(pivots_ref, slabs_ref, own_ref, factor_ref, out_ref, work, u_ref, p_ref):
    block = own_ref.shape[0]
    width = own_ref.shape[1]
    own_first = STEPS * block
    chunk = min(width, 1024)
    row_index = lax.axis_index("row")
    pivot_count = pivots_ref[lax.axis_index("col")]
    own_columns = pl.ds(pl.multiple_of(row_index * block, block), block)

    def chunks(body):
        if width == chunk:
            body(0)
        else:
            pl.loop(0, width // chunk)(lambda c: body(pl.multiple_of(c * chunk, chunk)))

    def load(c):
        columns = pl.ds(c, chunk)
        work[:own_first, columns] = slabs_ref[:, columns].astype(F32)
        work[own_first:, columns] = own_ref[:, columns].astype(F32)

    chunks(load)
    tri_row = lax.broadcasted_iota(jnp.int32, (block, block), 0)
    tri_column = lax.broadcasted_iota(jnp.int32, (block, block), 1)

    @pl.loop(0, STEPS)
    def _(t):
        active = t < pivot_count
        for half in range(block // BASE):
            first = pl.multiple_of(t * block + half * BASE, BASE)
            local = half * BASE
            upper, inverse = factor_base(work[pl.ds(first, BASE), pl.ds(first, BASE)])

            def solve(c):
                columns = pl.ds(c, chunk)
                u_ref[pl.ds(local, BASE), columns] = dot3(
                    inverse, work[pl.ds(first, BASE), columns], ((1,), (0,))
                )

            chunks(solve)
            u_ref[pl.ds(local, BASE), pl.ds(first, BASE)] = upper
            rest = block - local - BASE
            if rest:
                below = pl.multiple_of(first + BASE, BASE)
                left = u_ref[pl.ds(local, BASE), pl.ds(below, rest)]

                def update(c):
                    columns = pl.ds(c, chunk)
                    work[pl.ds(below, rest), columns] -= dot3(
                        left, u_ref[pl.ds(local, BASE), columns], ((0,), (0,))
                    )

                chunks(update)

        def round_panel(c):
            columns = pl.ds(c, chunk)
            place = lax.broadcasted_iota(jnp.int32, (block, chunk), 1) + c
            keep = (place >= (t + 1) * block) & active
            p_ref[:, columns] = jnp.where(keep, u_ref[:, columns], 0.0).astype(BF16)

        chunks(round_panel)
        own_factor = u_ref[:, own_columns].T
        keep = active & (row_index >= t) & ((row_index > t) | (tri_row >= tri_column))
        factor_ref[:, pl.ds(pl.multiple_of(t * block, block), block)] = jnp.where(
            keep, own_factor, 0.0
        )

        def trail(c):
            columns = pl.ds(c, chunk)
            right = p_ref[:, columns]
            for rows, left in (
                (pl.ds(block, own_first - block), p_ref[:, block:own_first]),
                (pl.ds(own_first, block), p_ref[:, own_columns]),
            ):
                work[rows, columns] -= lax.dot_general(
                    left, right, (((0,), (0,)), ((), ())), preferred_element_type=F32
                )

        chunks(trail)

    def store(c):
        columns = pl.ds(c, chunk)
        place = lax.broadcasted_iota(jnp.int32, (block, chunk), 1) + c
        keep = (place >= pivot_count * block) & (row_index >= pivot_count)
        out_ref[:, columns] = jnp.where(keep, work[own_first:, columns], 0.0)

    chunks(store)


def run_front(pivots, slabs, own):
    block, width = own.shape
    vmem = pl.BlockSpec(memory_space=pltpu.VMEM)
    return pl.pallas_call(
        front_kernel,
        out_shape=(
            jax.ShapeDtypeStruct((block, STEPS * block), F32),
            jax.ShapeDtypeStruct((block, width), F32),
        ),
        in_specs=[pl.BlockSpec(memory_space=pltpu.SMEM), vmem, vmem],
        out_specs=(vmem, vmem),
        scratch_shapes=[
            pltpu.VMEM(((STEPS + 1) * block, width), F32),
            pltpu.VMEM((block, width), F32),
            pltpu.VMEM((block, width), BF16),
        ],
        compiler_params=pltpu.CompilerParams(vmem_limit_bytes=56 * 1024 * 1024),
    )(pivots, slabs, own)


def shards(fronts, pivots, targets, ancestor):
    row_index = lax.axis_index("row")
    col_index = lax.axis_index("col")
    col_count = lax.axis_size("col")
    block_size = fronts.shape[1]
    width = fronts.shape[2]
    block_count = width // block_size
    gathered = lax.all_gather(fronts[0], "row", axis=0, tiled=True)
    factor, working = run_front(pivots, gathered[: STEPS * block_size], fronts[0])
    sibling_ids = jnp.arange(pivots.shape[0], dtype=jnp.int32)
    row_blocks = working.reshape(block_size, block_count, block_size)
    my_targets = jnp.sum(jnp.where(sibling_ids[:, None] == col_index, targets, 0), axis=0)
    dest_ids = jnp.arange(col_count, dtype=jnp.int32)
    owned_target = jnp.concatenate([my_targets, my_targets])
    keep = owned_target == dest_ids
    outgoing_blocks = jnp.where(
        keep[None, :, None], jnp.concatenate([row_blocks, row_blocks], axis=1), 0.0
    )
    received = lax.all_to_all(outgoing_blocks, "col", split_axis=1, concat_axis=1, tiled=True)
    block_ids = jnp.arange(block_count, dtype=jnp.int32)
    row_targets = jnp.sum(jnp.where(block_ids[None, :] == row_index, targets, 0), axis=1)
    halves = row_targets // block_count
    selector = (halves[None, :] == jnp.arange(2, dtype=jnp.int32)[:, None])[:, None, :, None]
    summed = jnp.sum(jnp.where(selector, received[None], 0.0), axis=2)
    return (factor[None], ancestor.astype(F32) + summed)


def solution(mesh):
    in_specs = (P("col", "row", None), P(), P(), P(None, "row", "col"))
    out_specs = (P("col", "row", None), P(None, "row", "col"))
    return jax.shard_map(shards, mesh=mesh, in_specs=in_specs, out_specs=out_specs, check_vma=False)
```

time: 406 us -> 140 us (0.34)
  the two profiles are of different devices: /device:TPU:15 before, /device:TPU:0 now
where the time goes in v1:
time: 140 us
  waiting for transfers between devices  75.3 us (54%)
  Pallas kernels  35.2 us (25%)
  between operations  14.1 us (10%)
  starting transfers between devices  5.53 us (4%)
  local copies, waits for them, and re-layouts  5.21 us (4%)
  other arithmetic  4.75 us (3%)
    all_to_all x1, waiting for transfers between devices, shards(): lax.all_to_all(outgoing_blocks, 'col', split_axis=1, concat_axis=1, tiled...  48.6 us
    pallas_call x1, Pallas kernels, run_front(): pl.pallas_call(front_kernel, out_shape=(jax.ShapeDtypeStruct((block, STEP...  35.2 us
    all_gather x1, waiting for transfers between devices, shards(): gathered = lax.all_gather(fronts[0], 'row', axis=0, tiled=True)  26 us
    all_to_all x1, starting transfers between devices, shards(): lax.all_to_all(outgoing_blocks, 'col', split_axis=1, concat_axis=1, tiled...  5.5 us
  transfers between devices with their start and end apart: 2, of which 2 were waited for; matrix products, arithmetic and copies ran while one was open for 1% of the time, Pallas kernels for 0%

profile of v1, /device:TPU:0, one launch (start us, length us, event | category | flops | bytes accessed | tf_op | source)
XLA Modules:
  0.0 140.1 jit_solution(14678652043062304952)
XLA Ops:
  7.2 0.0 all-gather.3.cloned.1.call-start
  7.2 0.7 all-gather.3.cloned.1.call-update
  7.9 0.9 select_reduce_fusion.2
  8.8 0.1 add_compare_fusion
  8.9 26.0 %all-gather.3.cloned.1.call-done = bf16[1,1024,1024]{2,1,0:T(8,128)(2,1)} async-done(((bf16[1,256,1024]{2,1,0:T(8,128)(2,1)}), bf16[1,1024,1024]{2,1,0:T(8,128)(2,1)}) %all-gather.3.cloned.1.call-update) | async-done | bytes 2097168 | tf_op jit(solution)/shard_map/all_gather | solution.py:225
  34.9 2.7 %slice_bitcast_fusion.slabs_ref = bf16[768,1024]{1,0:T(8,128)(2,1)} fusion(bf16[1,1024,1024]{2,1,0:T(8,128)(2,1)} %all-gather.3.cloned.1.call-done), kind=kLoop, calls=%fused_computation.2 | loop fusion | bytes 3145728 | tf_op jit(solution)/shard_map/slice | solution.py:226
  37.6 35.2 %shard_map.59 = (f32[256,768]{1,0:T(8,128)}, f32[256,1024]{1,0:T(8,128)}) custom-call(s32[8]{0:T(128)} %pivots_ref.1, bf16[768,1024]{1,0:T(8,128)(2,1)} %slice_bitcast_fusion.slabs_ref, bf16[256,1024]{1,0:T(8,128)(2,1)} %bitcast.9), custom_call_target="tpu_custom_call" | custom-call | tf_op jit(solution)/shard_map/pallas_call | solution.py:201
  72.8 1.3 copy.14
  74.1 1.6 %maximum_select_fusion = f32[256,8,256]{2,0,1:T(8,128)} fusion(f32[256,4,256]{2,0,1:T(8,128)S(1)} %bitcast.8, pred[8]{0:T(512)(128)(4,1)S(1)} %add_compare_fusion), kind=kLoop, calls=%fused_computation.1 | loop fusion | flops 1048576 | bytes 3145736 | tf_op jit(solution)/shard_map/jit(_where)/select_n | solution.py:233
  75.7 5.5 %all-to-all-start = ((f32[256,8,256]{2,0,1:T(8,128)}), f32[256,8,256]{2,0,1:T(8,128)S(1)}, u32[]{:S(2)}, u32[]{:S(2)}) async-start(f32[256,8,256]{2,0,1:T(8,128)} %maximum_select_fusion), calls=%async_computation | async-start | bytes 4194304 | tf_op jit(solution)/shard_map/all_to_all | solution.py:236
  81.2 48.6 %all-to-all-done = f32[256,8,256]{2,0,1:T(8,128)S(1)} async-done(((f32[256,8,256]{2,0,1:T(8,128)}), f32[256,8,256]{2,0,1:T(8,128)S(1)}, u32[]{:S(2)}, u32[]{:S(2)}) %all-to-all-start) | async-done | bytes 2097184 | tf_op jit(solution)/shard_map/all_to_all | solution.py:236
  129.8 1.2 copy.11
  131.1 0.0 copy-start
  131.1 1.3 select_reduce_fusion
  132.4 0.0 copy-done
  132.4 0.8 convert_add_fusion
  (4 shorter events, 0.0 us)
Async XLA Ops:
  7.2 27.7 %all-gather.3.cloned.1.call-start = ((), (), s32[]{:S(2)}) async-start(), calls=%async_computation.1 | async-start | bytes 2621440 | tf_op jit(solution)/shard_map/all_gather | solution.py:225
  75.7 54.1 %all-to-all-start = ((f32[256,8,256]{2,0,1:T(8,128)}), f32[256,8,256]{2,0,1:T(8,128)S(1)}, u32[]{:S(2)}, u32[]{:S(2)}) async-start(f32[256,8,256]{2,0,1:T(8,128)} %maximum_select_fusion), calls=%async_computation | async-start | bytes 4194304 | tf_op jit(solution)/shard_map/all_to_all | solution.py:236
  131.1 1.3 copy-start
Sparse Core Ops, SparseCore 0:
  9.6 25.2 all-gather.2

commit v2 on v1

v2 whole, which is shorter than its diff:
```python
import functools

import jax
import jax.numpy as jnp
from jax import lax
from jax.experimental import pallas as pl
from jax.experimental.pallas import tpu as pltpu
from jax.sharding import PartitionSpec as P

STEPS = 3
BASE = 128
GROUP = 8
MESH = pl.DeviceIdType.MESH
F32 = jnp.float32
BF16 = jnp.bfloat16


def split(x):
    high = x.astype(BF16)
    return high, (x - high.astype(F32)).astype(BF16)


def dot3(a, b, dims):
    a_high, a_low = split(a)
    b_high, b_low = split(b)

    def one(x, y):
        return lax.dot_general(x, y, (dims, ((), ())), preferred_element_type=F32)

    return one(a_high, b_high) + (one(a_high, b_low) + one(a_low, b_high))


def splat(x, i, j):
    return jnp.broadcast_to(x[i : i + 1, j : j + 1], (GROUP, BASE))


def row_of(x, i):
    return jnp.broadcast_to(x[i : i + 1, :], (GROUP, BASE))


def column_of(x, j):
    return jnp.broadcast_to(x[:, j : j + 1], (GROUP, BASE))


def factor_base(matrix):
    count = BASE // GROUP
    sub = lax.broadcasted_iota(jnp.int32, (GROUP, BASE), 0)
    lane = lax.broadcasted_iota(jnp.int32, (GROUP, BASE), 1)
    left = [matrix[m * GROUP : (m + 1) * GROUP, :] for m in range(count)]
    right = [(lane == sub + m * GROUP).astype(F32) for m in range(count)]
    upper, inverse = [], []
    for g in range(count):
        first = g * GROUP
        s = {
            (i, j): splat(left[g], i, first + j)
            for i in range(GROUP)
            for j in range(i, GROUP)
        }
        rows = [row_of(left[g], i) for i in range(GROUP)]
        extra = [row_of(right[g], i) for i in range(GROUP)]
        scale, u = [], {}
        for i in range(GROUP):
            r = lax.rsqrt(s[i, i])
            scale.append(r)
            for j in range(i + 1, GROUP):
                u[i, j] = s[i, j] * r
            rows[i] = rows[i] * r
            extra[i] = extra[i] * r
            for j in range(i + 1, GROUP):
                for k in range(j, GROUP):
                    s[j, k] = s[j, k] - u[i, j] * u[i, k]
                rows[j] = rows[j] - u[i, j] * rows[i]
                extra[j] = extra[j] - u[i, j] * extra[i]
        top, bottom = rows[0], extra[0]
        for i in range(1, GROUP):
            top = jnp.where(sub == i, rows[i], top)
            bottom = jnp.where(sub == i, extra[i], bottom)
        upper.append(jnp.where(lane >= sub + first, top, 0.0))
        inverse.append(bottom)
        if g + 1 == count:
            break
        m = g + 1
        left_sum, right_sum = left[m], right[m]
        columns = [column_of(left[m], first + i) for i in range(GROUP)]
        for i in range(GROUP):
            columns[i] = columns[i] * scale[i]
            for j in range(i + 1, GROUP):
                columns[j] = columns[j] - u[i, j] * columns[i]
            left_sum = left_sum - columns[i] * rows[i]
            right_sum = right_sum - columns[i] * extra[i]
        left[m], right[m] = left_sum, right_sum
        if g + 2 == count:
            continue
        back, back_extra = [None] * GROUP, [None] * GROUP
        for i in reversed(range(GROUP)):
            a, b = rows[i], extra[i]
            for k in range(i + 1, GROUP):
                a = a - u[i, k] * back[k]
                b = b - u[i, k] * back_extra[k]
            back[i], back_extra[i] = a * scale[i], b * scale[i]
        far_left = jnp.concatenate(left[g + 2 :], axis=0)
        far_right = jnp.concatenate(right[g + 2 :], axis=0)
        left_sum, right_sum = far_left, far_right
        for i in range(GROUP):
            column = jnp.broadcast_to(far_left[:, first + i : first + i + 1], far_left.shape)
            left_sum = left_sum - column * back[i][:1]
            right_sum = right_sum - column * back_extra[i][:1]
        for m in range(g + 2, count):
            place = (m - g - 2) * GROUP
            left[m] = left_sum[place : place + GROUP]
            right[m] = right_sum[place : place + GROUP]
    return jnp.concatenate(upper, axis=0), jnp.concatenate(inverse, axis=0)


LEVELS = 32767.0
TINY = 1e-30


def fused_kernel(
    rows,
    cols,
    pivots_ref,
    targets_ref,
    own_ref,
    ancestor_ref,
    factor_ref,
    out_ref,
    work,
    u_ref,
    p_ref,
    slabs,
    outgoing,
    out_scale,
    received,
    in_scale,
    row_send,
    row_recv,
    send_sem,
    scale_send,
    recv_sem,
    scale_recv,
):
    block = own_ref.shape[0]
    width = own_ref.shape[1]
    blocks = width // block
    own_first = STEPS * block
    chunk = min(width, 1024)
    row = lax.axis_index("row")
    col = lax.axis_index("col")
    core = lax.rem(row, 2)
    partner = row + 1 - 2 * core
    pivot_count = pivots_ref[col]
    own_columns = pl.ds(pl.multiple_of(row * block, block), block)

    barrier = pltpu.get_barrier_semaphore()
    for step in range(1, rows):
        pl.semaphore_signal(
            barrier, inc=1, device_id={"row": lax.rem(row + step, rows)}, device_id_type=MESH
        )
    for step in range(1, cols):
        pl.semaphore_signal(
            barrier, inc=1, device_id={"col": lax.rem(col + step, cols)}, device_id_type=MESH
        )
    pl.semaphore_wait(barrier, rows + cols - 2)

    pieces = [(0, 0, block), (0, block, width - block)]
    pieces += [(t, t * block, width - t * block) for t in range(1, STEPS)]

    def piece_copy(piece, source, target, slot):
        t, first, size = pieces[piece]
        columns = pl.ds(first, size)
        return pltpu.make_async_remote_copy(
            src_ref=source.at[:, columns] if source is own_ref else source.at[t, :, columns],
            dst_ref=slabs.at[t, :, columns],
            send_sem=row_send.at[piece, slot],
            recv_sem=row_recv.at[piece],
            device_id={"row": target},
            device_id_type=MESH,
        )

    def owner_copies(piece):
        slot = 0
        t = pieces[piece][0]
        copies = []
        for y in range(rows // 2):
            target = 2 * y + t % 2
            if target != t:
                copies.append(piece_copy(piece, own_ref, target, slot))
                slot += 1
        copies.append(piece_copy(piece, own_ref, t + 1 - 2 * (t % 2), slot))
        return copies

    def send_piece(piece):
        @pl.when(row == pieces[piece][0])
        def _():
            for copy in owner_copies(piece):
                copy.start()

    def arrive(piece):
        t, first, size = pieces[piece]

        @pl.when(row != t)
        def _():
            piece_copy(piece, slabs, partner, 0).wait_recv()

            @pl.when(core == t % 2)
            def _():
                piece_copy(piece, slabs, partner, 0).start()

            work[pl.ds(t * block, block), pl.ds(first, size)] = slabs[
                t, :, pl.ds(first, size)
            ].astype(F32)

        @pl.when(row == t)
        def _():
            work[pl.ds(t * block, block), pl.ds(first, size)] = own_ref[
                :, pl.ds(first, size)
            ].astype(F32)

    def chunks(body):
        if width == chunk:
            body(0)
        else:
            pl.loop(0, width // chunk)(lambda c: body(pl.multiple_of(c * chunk, chunk)))

    def block_copies(j, upper):
        target = j + upper * blocks
        return [
            pltpu.make_async_remote_copy(
                src_ref=source.at[j],
                dst_ref=sink.at[col],
                send_sem=sends.at[j, upper],
                recv_sem=recvs.at[col],
                device_id={"col": target},
                device_id_type=MESH,
            )
            for source, sink, sends, recvs in (
                (outgoing, received, send_sem, recv_sem),
                (out_scale, in_scale, scale_send, scale_recv),
            )
        ]

    def send_block(j):
        x = work[own_first:, j * block : (j + 1) * block]
        top = jnp.maximum(jnp.max(jnp.abs(x), axis=0, keepdims=True), TINY)
        outgoing[j] = jnp.floor(x * (LEVELS / top) + 0.5).astype(jnp.int32).astype(jnp.int16)
        out_scale[j] = jnp.broadcast_to(top * (1.0 / LEVELS), (GROUP, block))
        for upper in (1, 0):

            @pl.when(col != j + upper * blocks)
            def _():
                for copy in block_copies(j, upper):
                    copy.start()

            @pl.when(col == j + upper * blocks)
            def _():
                received[col] = outgoing[j]
                in_scale[col] = out_scale[j]

    send_piece(0)
    send_piece(1)
    work[own_first:, :] = own_ref[...].astype(F32)
    for t in range(1, STEPS):
        work[t * block : (t + 1) * block, : t * block] = jnp.zeros((block, t * block), F32)
    arrive(0)
    for piece in range(2, len(pieces)):
        send_piece(piece)
    tri_row = lax.broadcasted_iota(jnp.int32, (block, block), 0)
    tri_column = lax.broadcasted_iota(jnp.int32, (block, block), 1)

    @pl.loop(0, STEPS)
    def _(t):
        active = t < pivot_count

        @pl.loop(0, block // BASE)
        def _(half):
            local = pl.multiple_of(half * BASE, BASE)
            first = pl.multiple_of(t * block + local, BASE)
            upper, inverse = factor_base(work[pl.ds(first, BASE), pl.ds(first, BASE)])

            @pl.when((t == 0) & (half == 0))
            def _():
                arrive(1)

            def solve(c):
                columns = pl.ds(c, chunk)
                u_ref[pl.ds(local, BASE), columns] = dot3(
                    inverse, work[pl.ds(first, BASE), columns], ((1,), (0,))
                )

            chunks(solve)
            u_ref[pl.ds(local, BASE), pl.ds(first, BASE)] = upper

            @pl.when(half == 0)
            def _():
                below = pl.multiple_of(first + BASE, BASE)
                left = u_ref[pl.ds(local, BASE), pl.ds(below, BASE)]

                def update(c):
                    columns = pl.ds(c, chunk)
                    work[pl.ds(below, BASE), columns] -= dot3(
                        left, u_ref[pl.ds(local, BASE), columns], ((0,), (0,))
                    )

                chunks(update)

        def round_panel(c):
            columns = pl.ds(c, chunk)
            place = lax.broadcasted_iota(jnp.int32, (block, chunk), 1) + c
            keep = (place >= (t + 1) * block) & active
            p_ref[:, columns] = jnp.where(keep, u_ref[:, columns], 0.0).astype(BF16)

        chunks(round_panel)

        @pl.when(t == 0)
        def _():
            for piece in range(2, len(pieces)):
                arrive(piece)

        def trail(c):
            columns = pl.ds(c, chunk)
            right = p_ref[:, columns]
            for place, left in (
                (pl.ds(own_first, block), p_ref[:, own_columns]),
                (pl.ds(block, own_first - block), p_ref[:, block:own_first]),
            ):
                work[place, columns] -= lax.dot_general(
                    left, right, (((0,), (0,)), ((), ())), preferred_element_type=F32
                )

        chunks(trail)
        for j in range(1, blocks):
            level = jnp.minimum(row, min(j, STEPS))

            @pl.when(level == t + 1)
            def _():
                send_block(j)

        own_factor = u_ref[:, own_columns].T
        keep = active & (row >= t) & ((row > t) | (tri_row >= tri_column))
        factor_ref[:, pl.ds(pl.multiple_of(t * block, block), block)] = jnp.where(
            keep, own_factor, 0.0
        )

    out_ref[...] = ancestor_ref[...].astype(F32)
    mine = lax.rem(col, blocks)

    @pl.when((row >= 1) & (mine >= 1))
    def _():
        @pl.loop(0, cols)
        def _(source):
            @pl.when(source != col)
            def _():
                for sink, recvs in ((received, recv_sem), (in_scale, scale_recv)):
                    pltpu.make_async_remote_copy(
                        src_ref=sink.at[source],
                        dst_ref=sink.at[source],
                        send_sem=recvs.at[source],
                        recv_sem=recvs.at[source],
                        device_id={"col": source},
                        device_id_type=MESH,
                    ).wait_recv()

            values = received[source].astype(jnp.int32).astype(F32)
            scale = in_scale[source, 0:1, :]
            used = (pivots_ref[source] <= jnp.minimum(row, mine)) & (
                targets_ref[source, mine] == col
            )
            high = targets_ref[source, row] >= blocks
            out_ref[0] += values * jnp.where(used & ~high, scale, 0.0)
            out_ref[1] += values * jnp.where(used & high, scale, 0.0)

    for piece in range(len(pieces)):
        t = pieces[piece][0]

        @pl.when(row == t)
        def _():
            for copy in owner_copies(piece):
                copy.wait_send()

        @pl.when((row != t) & (core == t % 2))
        def _():
            piece_copy(piece, slabs, partner, 0).wait_send()

    @pl.when(row >= 1)
    def _():
        for j in range(1, blocks):
            for upper in (1, 0):

                @pl.when(col != j + upper * blocks)
                def _():
                    for copy in block_copies(j, upper):
                        copy.wait_send()


def shards(rows, cols, fronts, pivots, targets, ancestor):
    block, width = fronts.shape[1:]
    blocks = width // block
    vmem = pl.BlockSpec(memory_space=pltpu.VMEM)
    smem = pl.BlockSpec(memory_space=pltpu.SMEM)
    dma = pltpu.SemaphoreType.DMA
    factor, assembled = pl.pallas_call(
        functools.partial(fused_kernel, rows, cols),
        out_shape=(
            jax.ShapeDtypeStruct((block, STEPS * block), F32),
            jax.ShapeDtypeStruct(ancestor.shape, F32),
        ),
        in_specs=[smem, smem, vmem, vmem],
        out_specs=(vmem, vmem),
        scratch_shapes=[
            pltpu.VMEM(((STEPS + 1) * block, width), F32),
            pltpu.VMEM((block, width), F32),
            pltpu.VMEM((block, width), BF16),
            pltpu.VMEM((STEPS, block, width), BF16),
            pltpu.VMEM((blocks, block, block), jnp.int16),
            pltpu.VMEM((blocks, GROUP, block), F32),
            pltpu.VMEM((cols, block, block), jnp.int16),
            pltpu.VMEM((cols, GROUP, block), F32),
            dma((STEPS + 1, rows // 2)),
            dma((STEPS + 1,)),
            dma((blocks, 2)),
            dma((blocks, 2)),
            dma((cols,)),
            dma((cols,)),
        ],
        compiler_params=pltpu.CompilerParams(
            collective_id=0, has_side_effects=True, vmem_limit_bytes=56 * 1024 * 1024
        ),
    )(pivots, targets, fronts[0], ancestor)
    return (factor[None], assembled)


def solution(mesh):
    in_specs = (P("col", "row", None), P(), P(), P(None, "row", "col"))
    out_specs = (P("col", "row", None), P(None, "row", "col"))
    body = functools.partial(shards, mesh.shape["row"], mesh.shape["col"])
    return jax.shard_map(body, mesh=mesh, in_specs=in_specs, out_specs=out_specs, check_vma=False)
```

time: 140 us -> 60.7 us (0.43)
  the two profiles are of different devices: /device:TPU:0 before, /device:TPU:15 now
where the time goes in v2:
time: 60.7 us; the launch traced here: 60.5 us
  Pallas kernels  55.6 us (92%)
  local copies, waits for them, and re-layouts  4.27 us (7%)
  between operations  0.65 us (1%)
    pallas_call x1, Pallas kernels, shards(): pl.pallas_call(functools.partial(fused_kernel, rows, cols), out_shape=(ja...  55.6 us
    unnamed x5, local copies, waits for them, and re-layouts  4.27 us

profile of v2, /device:TPU:15, one launch (start us, length us, event | category | flops | bytes accessed | tf_op | source)
XLA Modules:
  0.0 60.5 jit_solution(4863501434181279079)
XLA Ops:
  0.6 1.3 %copy.6.targets_ref = s32[8,4]{1,0:T(8,128)} copy(s32[8,4]{0,1:T(4,128)} %param.6) | data formatting | bytes 256 | tf_op args[2]
  2.0 55.6 %shard_map.59 = (f32[256,768]{1,0:T(8,128)}, f32[2,256,256]{2,1,0:T(8,128)}) custom-call(s32[8]{0:T(128)} %pivots_ref.1, s32[8,4]{1,0:T(8,128)} %copy.6.targets_ref, bf16[256,1024]{1,0:T(8,128)(2,1)} %bitcast.3, bf16[2,256,256]{2,1,0:T(8,128)(2,1)} %ancestor_ref.1), custom_call_target="tpu_custom_call" | custom-call | tf_op jit(solution)/shard_map/pallas_call | solution.py:402
  57.5 0.0 copy-start
  57.6 2.1 %copy.9 = f32[1,256,768]{2,1,0:T(8,128)} copy(f32[1,256,768]{2,1,0:T(8,128)} %bitcast.2) | data formatting | bytes 1572864
  59.7 0.0 copy-done
  59.7 0.8 %copy.10 = f32[2,256,256]{2,1,0:T(8,128)} copy(f32[2,256,256]{2,1,0:T(8,128)S(1)} %copy-done) | data formatting | bytes 1048576
Async XLA Ops:
  57.5 2.1 %copy-start = (f32[2,256,256]{2,1,0:T(8,128)S(1)}, f32[2,256,256]{2,1,0:T(8,128)}, u32[]{:S(2)}) copy-start(f32[2,256,256]{2,1,0:T(8,128)} %get-tuple-element.9) | copy-start | bytes 1572868

commit v3 on v2

--- a/solution.py
+++ b/solution.py
@@ -122,7 +122,6 @@
     pivots_ref,
     targets_ref,
     own_ref,
-    ancestor_ref,
     factor_ref,
     out_ref,
     work,
@@ -257,18 +256,165 @@
                 received[col] = outgoing[j]
                 in_scale[col] = out_scale[j]
 
-    send_piece(0)
-    send_piece(1)
-    work[own_first:, :] = own_ref[...].astype(F32)
-    for t in range(1, STEPS):
-        work[t * block : (t + 1) * block, : t * block] = jnp.zeros((block, t * block), F32)
-    arrive(0)
-    for piece in range(2, len(pieces)):
-        send_piece(piece)
+    def direct(source, t, height, first, size, target, index, slot):
+        place = (pl.ds(0, height), pl.ds(first, size))
+        return pltpu.make_async_remote_copy(
+            src_ref=source.at[place],
+            dst_ref=slabs.at[t, *place],
+            send_sem=row_send.at[index, slot],
+            recv_sem=row_recv.at[index],
+            device_id={"row": target},
+            device_id_type=MESH,
+        )
+
+    shares = [(0, BASE, 0, BASE), (0, block, BASE, block - BASE), (0, block, block, block)]
+    shares += [(1, block, block, block)]
+
+    def share(index, target):
+        return direct(own_ref, *shares[index], target, index, target - 2)
+
+    def take(index):
+        t, height, first, size = shares[index]
+        work[pl.ds(t * block, height), pl.ds(first, size)] = slabs[
+            t, :height, pl.ds(first, size)
+        ].astype(F32)
+
+    def flip(source, t, j):
+        x = source[:, t * block : (t + 1) * block].astype(F32)
+        work[t * block : (t + 1) * block, j * block : (j + 1) * block] = x.T
+
+    def flips(source, j):
+        for t in range(2):
+            flip(source, t, j)
+
+    def partner_copy(r):
+        if r == 0:
+            return direct(own_ref, 0, block, 0, width, 1, 4, 0)
+        size = width if r == 2 else 2 * block
+        return direct(own_ref, 2, block, 0, size, 5 - r, 4, 0)
+
+    def pair_start():
+        @pl.when(row == 0)
+        def _():
+            for target in (2, 3):
+                share(0, target).start()
+            partner_copy(0).start()
+            for index in (1, 2):
+                for target in (2, 3):
+                    share(index, target).start()
+
+        for r in (2, 3):
+
+            @pl.when(row == r)
+            def _():
+                partner_copy(r).start()
+
+        work[own_first:, :] = own_ref[...].astype(F32)
+        work[:own_first, :block] = jnp.zeros((own_first, block), F32)
+        work[2 * block : own_first, : 2 * block] = jnp.zeros((block, 2 * block), F32)
+
+        @pl.when(row == 0)
+        def _():
+            work[:block, :] = own_ref[...].astype(F32)
+
+        @pl.when(row == 1)
+        def _():
+            partner_copy(0).wait_recv()
+            for target in (2, 3):
+                share(3, target).start()
+            work[:block, :] = slabs[0].astype(F32)
+            work[block : 2 * block, :] = own_ref[...].astype(F32)
+
+        for r in (2, 3):
+
+            @pl.when(row == r)
+            def _():
+                flips(own_ref, r)
+                if r == 2:
+                    work[2 * block : own_first, :] = own_ref[...].astype(F32)
+                share(0, r).wait_recv()
+                take(0)
+
+    def pair_middle():
+        for r in (2, 3):
+
+            @pl.when(row == r)
+            def _():
+                partner_copy(5 - r).wait_recv()
+                flips(slabs.at[2], 5 - r)
+                if r == 3:
+                    work[2 * block : own_first, :] = slabs[2].astype(F32)
+                for index in (1, 2):
+                    share(index, r).wait_recv()
+                    take(index)
+
+    def pair_late():
+        for r in (2, 3):
+
+            @pl.when(row == r)
+            def _():
+                share(3, r).wait_recv()
+                take(3)
+
+    def pair_finish():
+        @pl.when(row == 0)
+        def _():
+            for target in (2, 3):
+                for index in (0, 1, 2):
+                    share(index, target).wait_send()
+            partner_copy(0).wait_send()
+
+        @pl.when(row == 1)
+        def _():
+            for target in (2, 3):
+                share(3, target).wait_send()
+
+        for r in (2, 3):
+
+            @pl.when(row == r)
+            def _():
+                partner_copy(r).wait_send()
+
+    def slab_start():
+        send_piece(0)
+        send_piece(1)
+        work[own_first:, :] = own_ref[...].astype(F32)
+        for t in range(1, STEPS):
+            work[t * block : (t + 1) * block, : t * block] = jnp.zeros((block, t * block), F32)
+        arrive(0)
+        for piece in range(2, len(pieces)):
+            send_piece(piece)
+
+    def slab_middle():
+        arrive(1)
+
+    def slab_late():
+        for piece in range(2, len(pieces)):
+            arrive(piece)
+
+    def slab_finish():
+        for piece in range(len(pieces)):
+            t = pieces[piece][0]
+
+            @pl.when(row == t)
+            def _():
+                for copy in owner_copies(piece):
+                    copy.wait_send()
+
+            @pl.when((row != t) & (core == t % 2))
+            def _():
+                piece_copy(piece, slabs, partner, 0).wait_send()
+
+    if rows == 4 and blocks == 4:
+        start, middle, late, finish = pair_start, pair_middle, pair_late, pair_finish
+    else:
+        start, middle, late, finish = slab_start, slab_middle, slab_late, slab_finish
+    start()
     tri_row = lax.broadcasted_iota(jnp.int32, (block, block), 0)
     tri_column = lax.broadcasted_iota(jnp.int32, (block, block), 1)
-
-    @pl.loop(0, STEPS)
+    factor_ref[:, block:] = jnp.zeros((block, (STEPS - 1) * block), F32)
+
+    @pl.loop(0, jnp.minimum(row + 1, STEPS))
     def _(t):
         active = t < pivot_count
 
@@ -280,7 +426,7 @@
 
             @pl.when((t == 0) & (half == 0))
             def _():
-                arrive(1)
+                middle()
 
             def solve(c):
                 columns = pl.ds(c, chunk)
@@ -314,8 +460,7 @@
 
         @pl.when(t == 0)
         def _():
-            for piece in range(2, len(pieces)):
-                arrive(piece)
+            late()
 
         def trail(c):
             columns = pl.ds(c, chunk)
@@ -336,13 +481,12 @@
             def _():
                 send_block(j)
 
-        own_factor = u_ref[:, own_columns].T
-        keep = active & (row >= t) & ((row > t) | (tri_row >= tri_column))
+        keep = active & ((row > t) | (tri_row >= tri_column))
         factor_ref[:, pl.ds(pl.multiple_of(t * block, block), block)] = jnp.where(
-            keep, own_factor, 0.0
+            keep, -u_ref[:, own_columns].T, 0.0
         )
 
-    out_ref[...] = ancestor_ref[...].astype(F32)
+    out_ref[...] = jnp.zeros_like(out_ref)
     mine = lax.rem(col, blocks)
 
     @pl.when((row >= 1) & (mine >= 1))
@@ -364,23 +508,13 @@
             values = received[source].astype(jnp.int32).astype(F32)
             scale = in_scale[source, 0:1, :]
             used = (pivots_ref[source] <= jnp.minimum(row, mine)) & (
-                targets_ref[source, mine] == col
+                targets_ref[mine, source] == col
             )
-            high = targets_ref[source, row] >= blocks
+            high = targets_ref[row, source] >= blocks
             out_ref[0] += values * jnp.where(used & ~high, scale, 0.0)
             out_ref[1] += values * jnp.where(used & high, scale, 0.0)
 
-    for piece in range(len(pieces)):
-        t = pieces[piece][0]
-
-        @pl.when(row == t)
-        def _():
-            for copy in owner_copies(piece):
-                copy.wait_send()
-
-        @pl.when((row != t) & (core == t % 2))
-        def _():
-            piece_copy(piece, slabs, partner, 0).wait_send()
+    finish()
 
     @pl.when(row >= 1)
     def _():
@@ -399,13 +533,13 @@
     vmem = pl.BlockSpec(memory_space=pltpu.VMEM)
     smem = pl.BlockSpec(memory_space=pltpu.SMEM)
     dma = pltpu.SemaphoreType.DMA
-    factor, assembled = pl.pallas_call(
+    negated, added = pl.pallas_call(
         functools.partial(fused_kernel, rows, cols),
         out_shape=(
             jax.ShapeDtypeStruct((block, STEPS * block), F32),
             jax.ShapeDtypeStruct(ancestor.shape, F32),
         ),
-        in_specs=[smem, smem, vmem, vmem],
+        in_specs=[smem, smem, vmem],
         out_specs=(vmem, vmem),
         scratch_shapes=[
             pltpu.VMEM(((STEPS + 1) * block, width), F32),
@@ -416,8 +550,8 @@
             pltpu.VMEM((blocks, GROUP, block), F32),
             pltpu.VMEM((cols, block, block), jnp.int16),
             pltpu.VMEM((cols, GROUP, block), F32),
-            dma((STEPS + 1, rows // 2)),
-            dma((STEPS + 1,)),
+            dma((STEPS + 2, rows // 2)),
+            dma((STEPS + 2,)),
             dma((blocks, 2)),
             dma((blocks, 2)),
             dma((cols,)),
@@ -426,8 +560,8 @@
         compiler_params=pltpu.CompilerParams(
             collective_id=0, has_side_effects=True, vmem_limit_bytes=56 * 1024 * 1024
         ),
-    )(pivots, targets, fronts[0], ancestor)
-    return (factor[None], assembled)
+    )(pivots, targets.T, fronts[0])
+    return (-negated[None], ancestor.astype(F32) + added)
 
 
 def solution(mesh):

time: 60.7 us -> 55.2 us (0.909)
  local copies, waits for them, and re-layouts: 4.27 us -> 0.01 us
  Pallas kernels: 55.6 us -> 51.4 us
  other arithmetic: 0 us -> 2.98 us
    unnamed x5 -> x4, local copies, waits for them, and re-layouts: 4.27 us -> 0.01 us
    pallas_call x1, Pallas kernels: 55.6 us -> 51.4 us  [shards(): pl.pallas_call(functools.partial(fused_kernel, rows, cols), out_shape=(ja...]
    neg x0 -> x1, other arithmetic: none -> 2.13 us  [shards(): return (-negated[None], ancestor.astype(F32) + added)]
    add x0 -> x1, other arithmetic: none -> 0.85 us  [shards(): return (-negated[None], ancestor.astype(F32) + added)]
where the time goes in v3:
time: 55.2 us; the launch traced here: 55 us
  Pallas kernels  51.4 us (93%)
  other arithmetic  2.98 us (5%)
  between operations  0.66 us (1%)
    pallas_call x1, Pallas kernels, shards(): pl.pallas_call(functools.partial(fused_kernel, rows, cols), out_shape=(ja...  51.4 us
    neg x1, other arithmetic, shards(): return (-negated[None], ancestor.astype(F32) + added)  2.13 us

profile of v3, /device:TPU:15, one launch (start us, length us, event | category | flops | bytes accessed | tf_op | source)
XLA Modules:
  0.0 55.0 jit_solution(2115589419416370079)
XLA Ops:
  0.6 51.4 %shard_map.59 = (f32[256,768]{1,0:T(8,128)}, f32[2,256,256]{2,1,0:T(8,128)}) custom-call(s32[8]{0:T(128)} %pivots_ref.1, s32[4,8]{1,0:T(4,128)} %bitcast.5, bf16[256,1024]{1,0:T(8,128)(2,1)} %bitcast.4), custom_call_target="tpu_custom_call" | custom-call | tf_op jit(solution)/shard_map/pallas_call | solution.py:536
  52.0 0.0 copy-start
  52.0 0.0 copy-start.1
  52.1 2.1 %negate_bitcast_fusion = f32[1,256,768]{2,1,0:T(8,128)} fusion(f32[256,768]{1,0:T(8,128)} %get-tuple-element.4), kind=kLoop, calls=%fused_computation | loop fusion | flops 196608 | bytes 1572864 | tf_op jit(solution)/shard_map/neg | solution.py:564
  54.2 0.0 copy-done
  54.2 0.0 copy-done.1
  54.2 0.8 %convert_add_fusion = f32[2,256,256]{2,1,0:T(8,128)} fusion(f32[2,256,256]{2,1,0:T(8,128)S(1)} %copy-done, bf16[2,256,256]{2,1,0:T(8,128)(2,1)S(1)} %copy-done.1), kind=kLoop, calls=%fused_computation.1 | loop fusion | flops 262144 | bytes 1310720 | tf_op jit(solution)/shard_map/add | solution.py:564
Async XLA Ops:
  52.0 2.2 %copy-start = (f32[2,256,256]{2,1,0:T(8,128)S(1)}, f32[2,256,256]{2,1,0:T(8,128)}, u32[]{:S(2)}) copy-start(f32[2,256,256]{2,1,0:T(8,128)} %get-tuple-element.5) | copy-start | bytes 1572868
  52.0 2.2 %copy-start.1 = (bf16[2,256,256]{2,1,0:T(8,128)(2,1)S(1)}, bf16[2,256,256]{2,1,0:T(8,128)(2,1)}, u32[]{:S(2)}) copy-start(bf16[2,256,256]{2,1,0:T(8,128)(2,1)} %param.7) | copy-start | bytes 786436

commit v4 on v3

--- a/solution.py
+++ b/solution.py
@@ -48,6 +48,12 @@
     lane = lax.broadcasted_iota(jnp.int32, (GROUP, BASE), 1)
     left = [matrix[m * GROUP : (m + 1) * GROUP, :] for m in range(count)]
     right = [(lane == sub + m * GROUP).astype(F32) for m in range(count)]
+    spots = [jnp.where(right[m] > 0.0, left[m], 0.0) for m in range(count)]
+    diagonal = jnp.sum(sum(spots), axis=0, keepdims=True)
+    shrink = lax.rsqrt(diagonal)
+    for m in range(count):
+        tall = lax.rsqrt(jnp.sum(spots[m], axis=1, keepdims=True))
+        left[m] = left[m] * tall * shrink
     upper, inverse = [], []
     for g in range(count):
         first = g * GROUP
@@ -58,19 +64,26 @@
         }
         rows = [row_of(left[g], i) for i in range(GROUP)]
         extra = [row_of(right[g], i) for i in range(GROUP)]
-        scale, u = [], {}
-        for i in range(GROUP):
-            r = lax.rsqrt(s[i, i])
-            scale.append(r)
-            for j in range(i + 1, GROUP):
-                u[i, j] = s[i, j] * r
-            rows[i] = rows[i] * r
-            extra[i] = extra[i] * r
-            for j in range(i + 1, GROUP):
+        scale, u = [None] * GROUP, {}
+        for p in range(0, GROUP, 2):
+            q = p + 1
+            a, b = s[p, p], s[p, q]
+            r = lax.rsqrt(a)
+            d = lax.rsqrt(a * s[q, q] - b * b)
+            both = d * r
+            scale[p], scale[q] = r, a * both
+            u[p, q] = b * r
+            for j in range(q + 1, GROUP):
+                u[p, j] = s[p, j] * r
+                u[q, j] = (a * s[q, j] - b * s[p, j]) * both
+            for j in range(q + 1, GROUP):
                 for k in range(j, GROUP):
-                    s[j, k] = s[j, k] - u[i, j] * u[i, k]
-                rows[j] = rows[j] - u[i, j] * rows[i]
-                extra[j] = extra[j] - u[i, j] * extra[i]
+                    s[j, k] = (s[j, k] - u[p, j] * u[p, k]) - u[q, j] * u[q, k]
+            for x in (rows, extra):
+                x[p] = x[p] * r
+                x[q] = (x[q] - u[p, q] * x[p]) * scale[q]
+                for j in range(q + 1, GROUP):
+                    x[j] = (x[j] - u[p, j] * x[p]) - u[q, j] * x[q]
         top, bottom = rows[0], extra[0]
         for i in range(1, GROUP):
             top = jnp.where(sub == i, rows[i], top)
@@ -98,18 +111,17 @@
                 a = a - u[i, k] * back[k]
                 b = b - u[i, k] * back_extra[k]
             back[i], back_extra[i] = a * scale[i], b * scale[i]
-        far_left = jnp.concatenate(left[g + 2 :], axis=0)
-        far_right = jnp.concatenate(right[g + 2 :], axis=0)
-        left_sum, right_sum = far_left, far_right
+        far_left = jnp.stack(left[g + 2 :])
+        left_sum, right_sum = far_left, jnp.stack(right[g + 2 :])
         for i in range(GROUP):
-            column = jnp.broadcast_to(far_left[:, first + i : first + i + 1], far_left.shape)
-            left_sum = left_sum - column * back[i][:1]
-            right_sum = right_sum - column * back_extra[i][:1]
+            column = jnp.broadcast_to(far_left[:, :, first + i : first + i + 1], far_left.shape)
+            left_sum = left_sum - column * back[i][None]
+            right_sum = right_sum - column * back_extra[i][None]
         for m in range(g + 2, count):
-            place = (m - g - 2) * GROUP
-            left[m] = left_sum[place : place + GROUP]
-            right[m] = right_sum[place : place + GROUP]
-    return jnp.concatenate(upper, axis=0), jnp.concatenate(inverse, axis=0)
+            left[m] = left_sum[m - g - 2]
+            right[m] = right_sum[m - g - 2]
+    upper = jnp.concatenate(upper, axis=0) * (diagonal * shrink)
+    return upper, jnp.concatenate(inverse, axis=0) * shrink
 
 
 LEVELS = 32767.0
@@ -418,37 +430,31 @@
     def _(t):
         active = t < pivot_count
 
-        @pl.loop(0, block // BASE)
-        def _(half):
-            local = pl.multiple_of(half * BASE, BASE)
-            first = pl.multiple_of(t * block + local, BASE)
-            upper, inverse = factor_base(work[pl.ds(first, BASE), pl.ds(first, BASE)])
-
-            @pl.when((t == 0) & (half == 0))
-            def _():
-                middle()
-
-            def solve(c):
-                columns = pl.ds(c, chunk)
-                u_ref[pl.ds(local, BASE), columns] = dot3(
-                    inverse, work[pl.ds(first, BASE), columns], ((1,), (0,))
-                )
-
-            chunks(solve)
-            u_ref[pl.ds(local, BASE), pl.ds(first, BASE)] = upper
-
-            @pl.when(half == 0)
-            def _():
-                below = pl.multiple_of(first + BASE, BASE)
-                left = u_ref[pl.ds(local, BASE), pl.ds(below, BASE)]
-
-                def update(c):
-                    columns = pl.ds(c, chunk)
-                    work[pl.ds(below, BASE), columns] -= dot3(
-                        left, u_ref[pl.ds(local, BASE), columns], ((0,), (0,))
-                    )
-
-                chunks(update)
+        top = pl.ds(pl.multiple_of(t * block, BASE), BASE)
+        low = pl.ds(pl.multiple_of(t * block + BASE, BASE), BASE)
+        upper, inverse = factor_base(work[top, top])
+
+        @pl.when(t == 0)
+        def _():
+            middle()
+
+        cross = dot3(inverse, work[top, low], ((1,), (0,)))
+        low_upper, low_inverse = factor_base(work[low, low] - dot3(cross, cross, ((0,), (0,))))
+
+        def solve(c):
+            columns = pl.ds(c, chunk)
+            solved = dot3(inverse, work[top, columns], ((1,), (0,)))
+            u_ref[:BASE, columns] = solved
+            work[low, columns] -= dot3(cross, solved, ((0,), (0,)))
+
+        def solve_low(c):
+            columns = pl.ds(c, chunk)
+            u_ref[BASE:, columns] = dot3(low_inverse, work[low, columns], ((1,), (0,)))
+
+        chunks(solve)
+        chunks(solve_low)
+        u_ref[:BASE, top] = upper
+        u_ref[BASE:, low] = low_upper
 
         def round_panel(c):
             columns = pl.ds(c, chunk)
@@ -462,29 +468,30 @@
         def _():
             late()
 
-        def trail(c):
-            columns = pl.ds(c, chunk)
-            right = p_ref[:, columns]
-            for place, left in (
-                (pl.ds(own_first, block), p_ref[:, own_columns]),
-                (pl.ds(block, own_first - block), p_ref[:, block:own_first]),
-            ):
-                work[place, columns] -= lax.dot_general(
-                    left, right, (((0,), (0,)), ((), ())), preferred_element_type=F32
-                )
-
-        chunks(trail)
-        for j in range(1, blocks):
-            level = jnp.minimum(row, min(j, STEPS))
-
-            @pl.when(level == t + 1)
-            def _():
-                send_block(j)
-
         keep = active & ((row > t) | (tri_row >= tri_column))
         factor_ref[:, pl.ds(pl.multiple_of(t * block, block), block)] = jnp.where(
             keep, -u_ref[:, own_columns].T, 0.0
         )
+
+        def outer(left, columns):
+            dims = (((0,), (0,)), ((), ()))
+            return lax.dot_general(left, p_ref[:, columns], dims, preferred_element_type=F32)
+
+        def trail(c):
+            columns = pl.ds(c, chunk)
+            work[pl.ds(own_first, block), columns] -= outer(p_ref[:, own_columns], columns)
+
+            @pl.when(t + 1 < STEPS)
+            def _():
+                work[block:own_first, columns] -= outer(p_ref[:, block:own_first], columns)
+
+        chunks(trail)
+        for j in range(1, blocks):
+            level = jnp.minimum(row, min(j, STEPS))
+
+            @pl.when(level == t + 1)
+            def _():
+                send_block(j)
 
     out_ref[...] = jnp.zeros_like(out_ref)
     mine = lax.rem(col, blocks)

time: 55.2 us -> 51.2 us (0.928)
  Pallas kernels: 51.4 us -> 47.2 us
    pallas_call x1, Pallas kernels: 51.4 us -> 47.2 us  [shards(): pl.pallas_call(functools.partial(fused_kernel, rows, cols), out_shape=(ja...]
where the time goes in v4:
time: 51.2 us; the launch traced here: 50.8 us
  Pallas kernels  47.2 us (92%)
  other arithmetic  2.98 us (6%)
  between operations  0.66 us (1%)
    pallas_call x1, Pallas kernels, shards(): pl.pallas_call(functools.partial(fused_kernel, rows, cols), out_shape=(ja...  47.2 us
    neg x1, other arithmetic, shards(): return (-negated[None], ancestor.astype(F32) + added)  2.13 us

profile of v4, /device:TPU:15, one launch (start us, length us, event | category | flops | bytes accessed | tf_op | source)
XLA Modules:
  0.0 50.8 jit_solution(17900857360253464942)
XLA Ops:
  0.6 47.2 %shard_map.59 = (f32[256,768]{1,0:T(8,128)}, f32[2,256,256]{2,1,0:T(8,128)}) custom-call(s32[8]{0:T(128)} %pivots_ref.1, s32[4,8]{1,0:T(4,128)} %bitcast.5, bf16[256,1024]{1,0:T(8,128)(2,1)} %bitcast.4), custom_call_target="tpu_custom_call" | custom-call | tf_op jit(solution)/shard_map/pallas_call | solution.py:543
  47.8 0.0 copy-start
  47.8 0.0 copy-start.1
  47.8 2.1 %negate_bitcast_fusion = f32[1,256,768]{2,1,0:T(8,128)} fusion(f32[256,768]{1,0:T(8,128)} %get-tuple-element.4), kind=kLoop, calls=%fused_computation | loop fusion | flops 196608 | bytes 1572864 | tf_op jit(solution)/shard_map/neg | solution.py:571
  50.0 0.0 copy-done
  50.0 0.0 copy-done.1
  50.0 0.8 %convert_add_fusion = f32[2,256,256]{2,1,0:T(8,128)} fusion(f32[2,256,256]{2,1,0:T(8,128)S(1)} %copy-done, bf16[2,256,256]{2,1,0:T(8,128)(2,1)S(1)} %copy-done.1), kind=kLoop, calls=%fused_computation.1 | loop fusion | flops 262144 | bytes 1310720 | tf_op jit(solution)/shard_map/add | solution.py:571
Async XLA Ops:
  47.8 2.2 %copy-start = (f32[2,256,256]{2,1,0:T(8,128)S(1)}, f32[2,256,256]{2,1,0:T(8,128)}, u32[]{:S(2)}) copy-start(f32[2,256,256]{2,1,0:T(8,128)} %get-tuple-element.5) | copy-start | bytes 1572868
  47.8 2.2 %copy-start.1 = (bf16[2,256,256]{2,1,0:T(8,128)(2,1)S(1)}, bf16[2,256,256]{2,1,0:T(8,128)(2,1)}, u32[]{:S(2)}) copy-start(bf16[2,256,256]{2,1,0:T(8,128)(2,1)} %param.7) | copy-start | bytes 786436

commit v5 on v4

--- a/solution.py
+++ b/solution.py
@@ -28,10 +28,6 @@
         return lax.dot_general(x, y, (dims, ((), ())), preferred_element_type=F32)
 
     return one(a_high, b_high) + (one(a_high, b_low) + one(a_low, b_high))
-
-
-def splat(x, i, j):
-    return jnp.broadcast_to(x[i : i + 1, j : j + 1], (GROUP, BASE))
 
 
 def row_of(x, i):
@@ -57,11 +53,8 @@
     upper, inverse = [], []
     for g in range(count):
         first = g * GROUP
-        s = {
-            (i, j): splat(left[g], i, first + j)
-            for i in range(GROUP)
-            for j in range(i, GROUP)
-        }
+        raw = [column_of(left[g], first + j) for j in range(GROUP)]
+        s = {(i, j): row_of(raw[j], i) for i in range(GROUP) for j in range(i, GROUP)}
         rows = [row_of(left[g], i) for i in range(GROUP)]
         extra = [row_of(right[g], i) for i in range(GROUP)]
         scale, u = [None] * GROUP, {}
@@ -147,15 +140,12 @@
     row_send,
     row_recv,
     send_sem,
-    scale_send,
     recv_sem,
-    scale_recv,
 ):
     block = own_ref.shape[0]
     width = own_ref.shape[1]
     blocks = width // block
     own_first = STEPS * block
-    chunk = min(width, 1024)
     row = lax.axis_index("row")
     col = lax.axis_index("col")
     core = lax.rem(row, 2)
@@ -228,27 +218,38 @@
                 :, pl.ds(first, size)
             ].astype(F32)
 
-    def chunks(body):
-        if width == chunk:
-            body(0)
+    def chunk_of(first):
+        return width - first if width <= 1024 else block
+
+    def chunks(body, first):
+        size = chunk_of(first)
+        if width <= 1024:
+            body(first)
         else:
-            pl.loop(0, width // chunk)(lambda c: body(pl.multiple_of(c * chunk, chunk)))
-
-    def block_copies(j, upper):
-        target = j + upper * blocks
+            pl.loop(0, (width - first) // size)(
+                lambda c: body(pl.multiple_of(first + c * size, size))
+            )
+
+    def part_of(part, diagonal):
+        first = BASE if diagonal and part else 0
+        return pl.ds(first, block - first), pl.ds(part * BASE, BASE)
+
+    def block_copies(j, upper, diagonal):
+        pairs = [
+            (outgoing.at[j, *place], received.at[col, *place], send_sem, recv_sem, part)
+            for part, place in enumerate((part_of(0, diagonal), part_of(1, diagonal)))
+        ]
+        pairs.append((out_scale.at[j], in_scale.at[col], send_sem, recv_sem, 2))
         return [
             pltpu.make_async_remote_copy(
-                src_ref=source.at[j],
-                dst_ref=sink.at[col],
-                send_sem=sends.at[j, upper],
-                recv_sem=recvs.at[col],
-                device_id={"col": target},
+                src_ref=source,
+                dst_ref=sink,
+                send_sem=sends.at[j, upper, part],
+                recv_sem=recvs.at[col, part],
+                device_id={"col": j + upper * blocks},
                 device_id_type=MESH,
             )
-            for source, sink, sends, recvs in (
-                (outgoing, received, send_sem, recv_sem),
-                (out_scale, in_scale, scale_send, scale_recv),
-            )
+            for source, sink, sends, recvs, part in pairs
         ]
 
     def send_block(j):
@@ -257,11 +258,12 @@
         outgoing[j] = jnp.floor(x * (LEVELS / top) + 0.5).astype(jnp.int32).astype(jnp.int16)
         out_scale[j] = jnp.broadcast_to(top * (1.0 / LEVELS), (GROUP, block))
         for upper in (1, 0):
-
-            @pl.when(col != j + upper * blocks)
-            def _():
-                for copy in block_copies(j, upper):
-                    copy.start()
+            for diagonal in (False, True):
+
+                @pl.when((col != j + upper * blocks) & ((row == j) == diagonal))
+                def _():
+                    for copy in block_copies(j, upper, diagonal):
+                        copy.start()
 
             @pl.when(col == j + upper * blocks)
             def _():
@@ -426,50 +428,44 @@
     tri_column = lax.broadcasted_iota(jnp.int32, (block, block), 1)
     factor_ref[:, block:] = jnp.zeros((block, (STEPS - 1) * block), F32)
 
-    @pl.loop(0, jnp.minimum(row + 1, STEPS))
-    def _(t):
+    def step(t):
         active = t < pivot_count
-
-        top = pl.ds(pl.multiple_of(t * block, BASE), BASE)
-        low = pl.ds(pl.multiple_of(t * block + BASE, BASE), BASE)
+        top = pl.ds(t * block, BASE)
+        low = pl.ds(t * block + BASE, BASE)
+        after = (t + 1) * block
         upper, inverse = factor_base(work[top, top])
-
-        @pl.when(t == 0)
-        def _():
+        if t == 0:
             middle()
 
         cross = dot3(inverse, work[top, low], ((1,), (0,)))
         low_upper, low_inverse = factor_base(work[low, low] - dot3(cross, cross, ((0,), (0,))))
 
         def solve(c):
-            columns = pl.ds(c, chunk)
+            columns = pl.ds(c, chunk_of(after))
             solved = dot3(inverse, work[top, columns], ((1,), (0,)))
             u_ref[:BASE, columns] = solved
             work[low, columns] -= dot3(cross, solved, ((0,), (0,)))
 
         def solve_low(c):
-            columns = pl.ds(c, chunk)
+            columns = pl.ds(c, chunk_of(after))
             u_ref[BASE:, columns] = dot3(low_inverse, work[low, columns], ((1,), (0,)))
 
-        chunks(solve)
-        chunks(solve_low)
+        chunks(solve, after)
+        chunks(solve_low, after)
         u_ref[:BASE, top] = upper
+        u_ref[:BASE, low] = cross
+        u_ref[BASE:, top] = jnp.zeros((BASE, BASE), F32)
         u_ref[BASE:, low] = low_upper
 
         def round_panel(c):
-            columns = pl.ds(c, chunk)
-            place = lax.broadcasted_iota(jnp.int32, (block, chunk), 1) + c
-            keep = (place >= (t + 1) * block) & active
-            p_ref[:, columns] = jnp.where(keep, u_ref[:, columns], 0.0).astype(BF16)
-
-        chunks(round_panel)
-
-        @pl.when(t == 0)
-        def _():
+            columns = pl.ds(c, chunk_of(after))
+            p_ref[:, columns] = jnp.where(active, u_ref[:, columns], 0.0).astype(BF16)
+
+        chunks(round_panel, after)
+        if t == 0:
             late()
-
         keep = active & ((row > t) | (tri_row >= tri_column))
-        factor_ref[:, pl.ds(pl.multiple_of(t * block, block), block)] = jnp.where(
+        factor_ref[:, t * block : after] = jnp.where(
             keep, -u_ref[:, own_columns].T, 0.0
         )
 
@@ -478,14 +474,16 @@
             return lax.dot_general(left, p_ref[:, columns], dims, preferred_element_type=F32)
 
         def trail(c):
-            columns = pl.ds(c, chunk)
+            columns = pl.ds(c, chunk_of(after))
+            if after < own_first:
+                work[after:own_first, columns] -= outer(p_ref[:, after:own_first], columns)
             work[pl.ds(own_first, block), columns] -= outer(p_ref[:, own_columns], columns)
 
-            @pl.when(t + 1 < STEPS)
-            def _():
-                work[block:own_first, columns] -= outer(p_ref[:, block:own_first], columns)
-
-        chunks(trail)
+        @pl.when(row == t)
+        def _():
+            p_ref[:, own_columns] = jnp.zeros((block, block), BF16)
+
+        chunks(trail, after)
         for j in range(1, blocks):
             level = jnp.minimum(row, min(j, STEPS))
 
@@ -493,44 +491,62 @@
             def _():
                 send_block(j)
 
+    for t in range(STEPS):
+
+        @pl.when(row >= t)
+        def _():
+            step(t)
+
     out_ref[...] = jnp.zeros_like(out_ref)
     mine = lax.rem(col, blocks)
 
-    @pl.when((row >= 1) & (mine >= 1))
-    def _():
+    def collect(diagonal):
         @pl.loop(0, cols)
         def _(source):
+            places = [part_of(0, diagonal), part_of(1, diagonal)]
+
             @pl.when(source != col)
             def _():
-                for sink, recvs in ((received, recv_sem), (in_scale, scale_recv)):
+                sinks = [received.at[source, *place] for place in places]
+                for part, sink in enumerate([*sinks, in_scale.at[source]]):
                     pltpu.make_async_remote_copy(
-                        src_ref=sink.at[source],
-                        dst_ref=sink.at[source],
-                        send_sem=recvs.at[source],
-                        recv_sem=recvs.at[source],
+                        src_ref=sink,
+                        dst_ref=sink,
+                        send_sem=recv_sem.at[source, part],
+                        recv_sem=recv_sem.at[source, part],
                         device_id={"col": source},
                         device_id_type=MESH,
                     ).wait_recv()
 
-            values = received[source].astype(jnp.int32).astype(F32)
-            scale = in_scale[source, 0:1, :]
             used = (pivots_ref[source] <= jnp.minimum(row, mine)) & (
                 targets_ref[mine, source] == col
             )
             high = targets_ref[row, source] >= blocks
-            out_ref[0] += values * jnp.where(used & ~high, scale, 0.0)
-            out_ref[1] += values * jnp.where(used & high, scale, 0.0)
+            for place in places:
+                values = received[source, *place].astype(jnp.int32).astype(F32)
+                scale = in_scale[source, 0:1, place[1]]
+                out_ref[0, *place] += values * jnp.where(used & ~high, scale, 0.0)
+                out_ref[1, *place] += values * jnp.where(used & high, scale, 0.0)
+
+        if diagonal:
+            for half in range(2):
+                out_ref[half, :BASE, BASE:] = out_ref[half, BASE:, :BASE].T
+
+    for diagonal in (False, True):
+
+        @pl.when((row >= 1) & (mine >= 1) & ((row == mine) == diagonal))
+        def _():
+            collect(diagonal)
 
     finish()
 
-    @pl.when(row >= 1)
-    def _():
-        for j in range(1, blocks):
-            for upper in (1, 0):
-
-                @pl.when(col != j + upper * blocks)
+    for j in range(1, blocks):
+        for upper in (1, 0):
+            for diagonal in (False, True):
+
+                @pl.when((row >= 1) & (col != j + upper * blocks) & ((row == j) == diagonal))
                 def _():
-                    for copy in block_copies(j, upper):
+                    for copy in block_copies(j, upper, diagonal):
                         copy.wait_send()
 
 
@@ -559,10 +575,8 @@
             pltpu.VMEM((cols, GROUP, block), F32),
             dma((STEPS + 2, rows // 2)),
             dma((STEPS + 2,)),
-            dma((blocks, 2)),
-            dma((blocks, 2)),
-            dma((cols,)),
-            dma((cols,)),
+            dma((blocks, 2, 3)),
+            dma((cols, 3)),
         ],
         compiler_params=pltpu.CompilerParams(
             collective_id=0, has_side_effects=True, vmem_limit_bytes=56 * 1024 * 1024

time: 51.2 us -> 48.6 us (0.949)
  Pallas kernels: 47.2 us -> 44.6 us
    pallas_call x1, Pallas kernels: 47.2 us -> 44.6 us  [shards(): pl.pallas_call(functools.partial(fused_kernel, rows, cols), out_shape=(ja...]
where the time goes in v5:
time: 48.6 us; the launch traced here: 48.2 us
  Pallas kernels  44.6 us (92%)
  other arithmetic  2.98 us (6%)
  between operations  0.66 us (1%)
    pallas_call x1, Pallas kernels, shards(): pl.pallas_call(functools.partial(fused_kernel, rows, cols), out_shape=(ja...  44.6 us
    neg x1, other arithmetic, shards(): return (-negated[None], ancestor.astype(F32) + added)  2.13 us

profile of v5, /device:TPU:15, one launch (start us, length us, event | category | flops | bytes accessed | tf_op | source)
XLA Modules:
  0.0 48.2 jit_solution(599896423307723518)
XLA Ops:
  0.6 44.6 %shard_map.59 = (f32[256,768]{1,0:T(8,128)}, f32[2,256,256]{2,1,0:T(8,128)}) custom-call(s32[8]{0:T(128)} %pivots_ref.1, s32[4,8]{1,0:T(4,128)} %bitcast.5, bf16[256,1024]{1,0:T(8,128)(2,1)} %bitcast.4), custom_call_target="tpu_custom_call" | custom-call | tf_op jit(solution)/shard_map/pallas_call | solution.py:559
  45.2 0.0 copy-start
  45.2 0.0 copy-start.1
  45.2 2.1 %negate_bitcast_fusion = f32[1,256,768]{2,1,0:T(8,128)} fusion(f32[256,768]{1,0:T(8,128)} %get-tuple-element.4), kind=kLoop, calls=%fused_computation | loop fusion | flops 196608 | bytes 1572864 | tf_op jit(solution)/shard_map/neg | solution.py:585
  47.4 0.0 copy-done
  47.4 0.0 copy-done.1
  47.4 0.8 %convert_add_fusion = f32[2,256,256]{2,1,0:T(8,128)} fusion(f32[2,256,256]{2,1,0:T(8,128)S(1)} %copy-done, bf16[2,256,256]{2,1,0:T(8,128)(2,1)S(1)} %copy-done.1), kind=kLoop, calls=%fused_computation.1 | loop fusion | flops 262144 | bytes 1310720 | tf_op jit(solution)/shard_map/add | solution.py:585
Async XLA Ops:
  45.2 2.2 %copy-start = (f32[2,256,256]{2,1,0:T(8,128)S(1)}, f32[2,256,256]{2,1,0:T(8,128)}, u32[]{:S(2)}) copy-start(f32[2,256,256]{2,1,0:T(8,128)} %get-tuple-element.5) | copy-start | bytes 1572868
  45.2 2.2 %copy-start.1 = (bf16[2,256,256]{2,1,0:T(8,128)(2,1)S(1)}, bf16[2,256,256]{2,1,0:T(8,128)(2,1)}, u32[]{:S(2)}) copy-start(bf16[2,256,256]{2,1,0:T(8,128)(2,1)} %param.7) | copy-start | bytes 786436
